TPU v7x, 512 devices: a whole 4x8x8 slice. The times are simulated.
512 devices in a mesh: row: 32 (over y, x), col: 16 (over z, core).
Axes of the slice: x: 4, y: 8, z: 8, core: 2. Of those that a mesh axis runs over, the one named last changes fastest.
Arguments:
- inputs: int32 [8, 128, 128], replicated, may hold values 0 or 1
- targets: int32 [8, 128, 128], replicated, may hold values 0 or 1
- initial_spikes: int32 [128, 128, 128], P(None, 'row'), may hold values 0 or 1
- w_in: bfloat16 [128, 128, 128], P(None, 'row'), may hold values from -0.5 to 0.5
- w_rec: bfloat16 [128, 128, 128, 128], P(None, 'col', 'row'), may hold values from -0.046875 to 0.046875
- w_out: bfloat16 [128, 128, 128], P('row'), may hold values from -0.046875 to 0.046875
- feedback: bfloat16 [128, 128, 128], P(None, 'row')
- adapt_gain: float32 [128, 128], P('row'), may hold values from 0.1 to 2
- adapt_decay: float32 [128, 128], P('row'), may hold values from 0.8 to 0.99
Outputs:
- readout: float32 [8, 128, 128], replicated
- grad_clipped: float32 [128, 128, 128, 128], P(None, 'col', 'row')
All inputs are finite; a program needn't handle non-finite values. No bound on the sum of `initial_spikes` on one device may be relied on, other than what follows from the above.
Results may differ from a plain program's by a relative error of at most 0.0015.
Values may be sent and summed in bfloat16 or wider, within the bound.
A program may use at most 128 MiB of HBM per device.

v0:
```python
import functools
import jax
import jax.numpy as jnp
from jax import lax
from jax.sharding import Mesh
from jax.sharding import PartitionSpec as P

NA = 128
NB = 128
COL = ("col_0", "col_1")
ROW = ("row_0", "row_1")
ROW_COL = ("row_0", "row_1", "col_0", "col_1")
cellular_leak_multiplier = 0.8
readout_decay = 0.8


def cut_along(array, dim, length):
    before, after = (array.shape[:dim], array.shape[dim + 1 :])
    return jnp.moveaxis(array.reshape(*before, length, -1, *after), dim, 0)


def sum_at_owner(array, axis, dim):
    length = lax.axis_size(axis)
    pieces = lax.all_to_all(cut_along(array, dim, length), axis, 0, 0, tiled=True)
    return jnp.sum(pieces, axis=0)


def laid_out(pieces, dim):
    shape = list(pieces.shape[1:])
    shape[dim] *= pieces.shape[0]
    return jnp.moveaxis(pieces, 0, dim).reshape(shape)


def sent_to_all(array, axis):
    copies = jnp.broadcast_to(array, (lax.axis_size(axis), *array.shape))
    return lax.all_to_all(copies, axis, split_axis=0, concat_axis=0, tiled=True)


def collect(array, axis, dim):
    return laid_out(sent_to_all(array, axis), dim)


def summed_rows(array, axes, dim):
    far, near = axes
    own = sum_at_owner(cut_along(array, dim, lax.axis_size(far)), near, dim + 1)
    return jnp.sum(lax.all_to_all(own, far, 0, 0, tiled=True), axis=0)


def rows_for(lines, length):
    spare = -lines.shape[0] % length
    if not spare:
        return lines
    return jnp.concatenate([lines, jnp.zeros((spare, *lines.shape[1:]), lines.dtype)])


def whole_of(array, axes, dim):
    far, near = axes
    pieces = sent_to_all(sent_to_all(array, far), near)
    return laid_out(pieces.swapaxes(0, 1).reshape(-1, *array.shape), dim)


def nested_sum(array, axes):
    lines = array.reshape(-1, array.shape[-1])
    own = summed_rows(rows_for(lines, lax.axis_size(axes[0]) * lax.axis_size(axes[1])), axes, 0)
    whole = whole_of(own, axes, 0)
    return whole[: len(lines)].reshape(array.shape)


def by_axis(array, axes):
    return functools.reduce(lax.psum, axes, array)


def body(inputs, targets, initial_spikes, w_in, w_rec, w_out, feedback, adapt_gain, adapt_decay):
    steps_count, batch, channels = inputs.shape
    own_cols = w_rec.shape[1]
    rows_loc = w_rec.shape[2]
    entire_column_set = w_rec.shape[3]
    col_start = lax.axis_index(COL) * own_cols
    rows_all = steps_count * batch

    def own_part(array, axis_dim):
        return lax.dynamic_slice_in_dim(array, col_start, own_cols, axis_dim)

    def select_cols(array, axis_dim):
        return own_part(array, axis_dim)

    def combine_currents(partial_value):
        return sum_at_owner(partial_value, COL, 2)

    weights = w_rec.reshape(w_rec.shape[0] * own_cols, rows_loc * entire_column_set)
    w_in_loc = select_cols(w_in, 2)
    state_cols = w_in_loc.shape[2]
    external = jnp.dot(
        inputs.reshape(rows_all, channels).astype(jnp.bfloat16),
        w_in_loc.reshape(channels, -1),
        preferred_element_type=jnp.float32,
    ).reshape(steps_count, batch, rows_loc, state_cols)
    coupling_magnitude = select_cols(adapt_gain, 1)
    retention = select_cols(adapt_decay, 1)
    start_spikes = select_cols(initial_spikes, 2).astype(jnp.bfloat16)

    def advance(state, drive_now):
        pulse_output, cellular_charge, barrier_shift_amount, sender_trace = state
        arrivals = collect(pulse_output, ROW, 1).reshape(batch, -1)
        sender_trace = cellular_leak_multiplier * sender_trace + arrivals.astype(jnp.float32)
        partial_value = jnp.dot(arrivals, weights, preferred_element_type=jnp.float32).reshape(
            batch, rows_loc, entire_column_set
        )
        current = drive_now + combine_currents(partial_value)
        spike_float = pulse_output.astype(jnp.float32)
        cellular_charge = cellular_leak_multiplier * cellular_charge + current - spike_float
        barrier_shift_amount = retention * barrier_shift_amount + spike_float
        present_emission_frequency = jax.nn.sigmoid(
            cellular_charge - 1.0 - coupling_magnitude * barrier_shift_amount
        )
        surrogate_slope = present_emission_frequency * (1.0 - present_emission_frequency)
        pulse_output = present_emission_frequency.astype(jnp.bfloat16)
        return (
            (pulse_output, cellular_charge, barrier_shift_amount, sender_trace),
            (sender_trace.astype(jnp.bfloat16), surrogate_slope, pulse_output),
        )

    zeros = jnp.zeros((batch, rows_loc, state_cols), jnp.float32)
    trace_zero = jnp.zeros((batch, weights.shape[0]), jnp.float32)
    _, (traces, slopes, spikes) = lax.scan(
        advance, (start_spikes, zeros, zeros, trace_zero), external
    )
    readout_loc = own_part(w_out, 1).reshape(rows_loc * own_cols, -1)
    projected = nested_sum(
        jnp.dot(spikes.reshape(rows_all, -1), readout_loc, preferred_element_type=jnp.float32),
        ("row_0", ("row_1", "col_0", "col_1")),
    )
    outputs_n = readout_loc.shape[1]
    projected = projected.reshape(steps_count, batch, outputs_n)

    def smooth(level, incoming):
        level = readout_decay * level + incoming
        return (level, level)

    _, readout = lax.scan(smooth, jnp.zeros((batch, outputs_n), jnp.float32), projected)
    errors = (jax.nn.sigmoid(readout) - targets.astype(jnp.float32)).reshape(rows_all, outputs_n)
    err_high = errors.astype(jnp.bfloat16)
    err_low = (errors - err_high.astype(jnp.float32)).astype(jnp.bfloat16)
    feedback_loc = select_cols(feedback, 2).reshape(outputs_n, -1)
    signal = jnp.dot(err_high, feedback_loc, preferred_element_type=jnp.float32) + jnp.dot(
        err_low, feedback_loc, preferred_element_type=jnp.float32
    )
    signal = signal.reshape(steps_count, batch, rows_loc, state_cols)
    weighted = signal * slopes
    decays = retention - slopes * coupling_magnitude

    def backward(carried, inputs_now):
        weighted_now, decay_now = inputs_now
        return (weighted_now + decay_now * carried, carried)

    _, future = lax.scan(backward, zeros, (weighted, decays), reverse=True)
    factors = (weighted - coupling_magnitude * slopes * future).astype(jnp.bfloat16)
    traces_flat = traces.reshape(rows_all, -1)
    pieces = lax.all_gather(
        factors.reshape(rows_all, rows_loc, state_cols), COL, axis=2, tiled=True
    )
    product = lax.dot_general(
        traces_flat,
        pieces.reshape(rows_all, -1),
        (((0,), (0,)), ((), ())),
        preferred_element_type=jnp.float32,
    )
    grad = product.reshape(-1, rows_loc, pieces.shape[2])
    squares = by_axis(jnp.sum(grad * grad), ROW_COL)
    clip_factor = jnp.minimum(1.0, NA * NB / 16.0 / jnp.sqrt(squares + 1e-06))
    return (readout, (grad * clip_factor).reshape(w_rec.shape))


def solution(mesh):
    finer = Mesh(mesh.devices.reshape(8, 4, 8, 2), ("row_0", "row_1", "col_0", "col_1"))
    placed = (
        P(),
        P(),
        P(None, ROW, None),
        P(None, ROW, None),
        P(None, COL, ROW, None),
        P(ROW, None, None),
        P(None, ROW, None),
        P(ROW, None),
        P(ROW, None),
    )
    return jax.shard_map(
        body, mesh=finer, in_specs=placed, out_specs=(P(), P(None, COL, ROW, None)), check_vma=False
    )
```

profile of v0, /device:TPU:1, one launch (start us, length us, event | category | flops | bytes accessed | tf_op | source)
XLA Modules:
  0.0 466.9 jit_solution(16170017238563502800)
XLA Ops:
  7.3 1.1 constant_dynamic-slice_fusion.4
  8.5 1.1 convert_element_type.57
  11.0 286.9 %while.55 = (s32[]{:T(128)}, bf16[128,4,8]{0,2,1:T(8,128)(2,1)S(1)}, f32[128,4,8]{0,2,1:T(8,128)S(1)}, f32[128,4,8]{0,2,1:T(8,128)S(1)}, f32[128,1024]{0,1:T(8,1...) while((s32[]{:T(128)}, ...), condition=%wide.region_2.3_spmd.clone, body=%wide.region_0.2_spmd.clone.sunk | while | flops 135032832 | bytes 6756560 | solution.py:125
  11.0 21.5 %all_to_all.41 = bf16[32,128,4,8]{1,3,2,0:T(8,128)(2,1)S(1)} all-to-all(bf16[32,128,4,8]{1,3,2,0:T(8,128)(2,1)S(1)} %broadcast_in_dim.84), channel_id=1, replica_groups=mesh['row_0'=8,'row_1'=4,'col_0'=8,'col_1'=2] {'row_0','row_1'}, dimensions={0} | all-to-all | bytes 524288 | tf_op jit(solution)/shard_map/while/body/eval_jaxpr/all_to_all | solution.py:36
  33.2 0.8 copy.144
  34.0 12.8 %all-to-all-start.1 = ((f32[16,128,4,8]{1,3,2,0:T(8,128)}), f32[16,128,4,8]{1,3,2,0:T(8,128)S(1)}, u32[]{:S(2)}, u32[]{:S(2)}) async-start(f32[16,128,4,8]{1,3,2,0:T(8,128)} %copy.144), calls=%async_computation.1 | async-start | bytes 524288 | tf_op jit(solution)/shard_map/while/body/eval_jaxpr/all_to_all | solution.py:24
  48.0 10.5 %all-to-all-done.1 = f32[16,128,4,8]{1,3,2,0:T(8,128)S(1)} async-done(((f32[16,128,4,8]{1,3,2,0:T(8,128)}), f32[16,128,4,8]{1,3,2,0:T(8,128)S(1)}, u32[]{:S(2)}, u32[]{:S(2)}) %all-to-all-start.1) | async-done | bytes 262176 | tf_op jit(solution)/shard_map/while/body/eval_jaxpr/all_to_all | solution.py:24
  58.8 16.4 %all_to_all.41 = bf16[32,128,4,8]{1,3,2,0:T(8,128)(2,1)S(1)} all-to-all(bf16[32,128,4,8]{1,3,2,0:T(8,128)(2,1)S(1)} %broadcast_in_dim.84), channel_id=1, replica_groups=mesh['row_0'=8,'row_1'=4,'col_0'=8,'col_1'=2] {'row_0','row_1'}, dimensions={0} | all-to-all | bytes 524288 | tf_op jit(solution)/shard_map/while/body/eval_jaxpr/all_to_all | solution.py:36
  75.9 0.8 copy.144
  76.7 4.0 all-to-all-start.1
  82.0 10.6 %all-to-all-done.1 = f32[16,128,4,8]{1,3,2,0:T(8,128)S(1)} async-done(((f32[16,128,4,8]{1,3,2,0:T(8,128)}), f32[16,128,4,8]{1,3,2,0:T(8,128)S(1)}, u32[]{:S(2)}, u32[]{:S(2)}) %all-to-all-start.1) | async-done | bytes 262176 | tf_op jit(solution)/shard_map/while/body/eval_jaxpr/all_to_all | solution.py:24
  92.9 16.7 %all_to_all.41 = bf16[32,128,4,8]{1,3,2,0:T(8,128)(2,1)S(1)} all-to-all(bf16[32,128,4,8]{1,3,2,0:T(8,128)(2,1)S(1)} %broadcast_in_dim.84), channel_id=1, replica_groups=mesh['row_0'=8,'row_1'=4,'col_0'=8,'col_1'=2] {'row_0','row_1'}, dimensions={0} | all-to-all | bytes 524288 | tf_op jit(solution)/shard_map/while/body/eval_jaxpr/all_to_all | solution.py:36
  110.2 0.8 copy.144
  111.0 3.7 all-to-all-start.1
  116.0 10.6 %all-to-all-done.1 = f32[16,128,4,8]{1,3,2,0:T(8,128)S(1)} async-done(((f32[16,128,4,8]{1,3,2,0:T(8,128)}), f32[16,128,4,8]{1,3,2,0:T(8,128)S(1)}, u32[]{:S(2)}, u32[]{:S(2)}) %all-to-all-start.1) | async-done | bytes 262176 | tf_op jit(solution)/shard_map/while/body/eval_jaxpr/all_to_all | solution.py:24
  126.9 16.9 %all_to_all.41 = bf16[32,128,4,8]{1,3,2,0:T(8,128)(2,1)S(1)} all-to-all(bf16[32,128,4,8]{1,3,2,0:T(8,128)(2,1)S(1)} %broadcast_in_dim.84), channel_id=1, replica_groups=mesh['row_0'=8,'row_1'=4,'col_0'=8,'col_1'=2] {'row_0','row_1'}, dimensions={0} | all-to-all | bytes 524288 | tf_op jit(solution)/shard_map/while/body/eval_jaxpr/all_to_all | solution.py:36
  144.4 0.8 copy.144
  145.2 3.7 all-to-all-start.1
  150.2 10.6 %all-to-all-done.1 = f32[16,128,4,8]{1,3,2,0:T(8,128)S(1)} async-done(((f32[16,128,4,8]{1,3,2,0:T(8,128)}), f32[16,128,4,8]{1,3,2,0:T(8,128)S(1)}, u32[]{:S(2)}, u32[]{:S(2)}) %all-to-all-start.1) | async-done | bytes 262176 | tf_op jit(solution)/shard_map/while/body/eval_jaxpr/all_to_all | solution.py:24
  161.1 16.9 %all_to_all.41 = bf16[32,128,4,8]{1,3,2,0:T(8,128)(2,1)S(1)} all-to-all(bf16[32,128,4,8]{1,3,2,0:T(8,128)(2,1)S(1)} %broadcast_in_dim.84), channel_id=1, replica_groups=mesh['row_0'=8,'row_1'=4,'col_0'=8,'col_1'=2] {'row_0','row_1'}, dimensions={0} | all-to-all | bytes 524288 | tf_op jit(solution)/shard_map/while/body/eval_jaxpr/all_to_all | solution.py:36
  178.6 0.8 copy.144
  179.4 3.7 all-to-all-start.1
  184.4 10.6 %all-to-all-done.1 = f32[16,128,4,8]{1,3,2,0:T(8,128)S(1)} async-done(((f32[16,128,4,8]{1,3,2,0:T(8,128)}), f32[16,128,4,8]{1,3,2,0:T(8,128)S(1)}, u32[]{:S(2)}, u32[]{:S(2)}) %all-to-all-start.1) | async-done | bytes 262176 | tf_op jit(solution)/shard_map/while/body/eval_jaxpr/all_to_all | solution.py:24
  195.3 16.9 %all_to_all.41 = bf16[32,128,4,8]{1,3,2,0:T(8,128)(2,1)S(1)} all-to-all(bf16[32,128,4,8]{1,3,2,0:T(8,128)(2,1)S(1)} %broadcast_in_dim.84), channel_id=1, replica_groups=mesh['row_0'=8,'row_1'=4,'col_0'=8,'col_1'=2] {'row_0','row_1'}, dimensions={0} | all-to-all | bytes 524288 | tf_op jit(solution)/shard_map/while/body/eval_jaxpr/all_to_all | solution.py:36
  213.6 3.7 all-to-all-start.1
  218.6 10.6 %all-to-all-done.1 = f32[16,128,4,8]{1,3,2,0:T(8,128)S(1)} async-done(((f32[16,128,4,8]{1,3,2,0:T(8,128)}), f32[16,128,4,8]{1,3,2,0:T(8,128)S(1)}, u32[]{:S(2)}, u32[]{:S(2)}) %all-to-all-start.1) | async-done | bytes 262176 | tf_op jit(solution)/shard_map/while/body/eval_jaxpr/all_to_all | solution.py:24
  229.5 16.9 %all_to_all.41 = bf16[32,128,4,8]{1,3,2,0:T(8,128)(2,1)S(1)} all-to-all(bf16[32,128,4,8]{1,3,2,0:T(8,128)(2,1)S(1)} %broadcast_in_dim.84), channel_id=1, replica_groups=mesh['row_0'=8,'row_1'=4,'col_0'=8,'col_1'=2] {'row_0','row_1'}, dimensions={0} | all-to-all | bytes 524288 | tf_op jit(solution)/shard_map/while/body/eval_jaxpr/all_to_all | solution.py:36
  247.8 3.7 all-to-all-start.1
  252.8 10.6 %all-to-all-done.1 = f32[16,128,4,8]{1,3,2,0:T(8,128)S(1)} async-done(((f32[16,128,4,8]{1,3,2,0:T(8,128)}), f32[16,128,4,8]{1,3,2,0:T(8,128)S(1)}, u32[]{:S(2)}, u32[]{:S(2)}) %all-to-all-start.1) | async-done | bytes 262176 | tf_op jit(solution)/shard_map/while/body/eval_jaxpr/all_to_all | solution.py:24
  263.7 16.9 %all_to_all.41 = bf16[32,128,4,8]{1,3,2,0:T(8,128)(2,1)S(1)} all-to-all(bf16[32,128,4,8]{1,3,2,0:T(8,128)(2,1)S(1)} %broadcast_in_dim.84), channel_id=1, replica_groups=mesh['row_0'=8,'row_1'=4,'col_0'=8,'col_1'=2] {'row_0','row_1'}, dimensions={0} | all-to-all | bytes 524288 | tf_op jit(solution)/shard_map/while/body/eval_jaxpr/all_to_all | solution.py:36
  282.0 3.7 all-to-all-start.1
  287.0 10.6 %all-to-all-done.1 = f32[16,128,4,8]{1,3,2,0:T(8,128)S(1)} async-done(((f32[16,128,4,8]{1,3,2,0:T(8,128)}), f32[16,128,4,8]{1,3,2,0:T(8,128)S(1)}, u32[]{:S(2)}, u32[]{:S(2)}) %all-to-all-start.1) | async-done | bytes 262176 | tf_op jit(solution)/shard_map/while/body/eval_jaxpr/all_to_all | solution.py:24
  297.9 0.9 copy.105
  299.3 0.9 convolution_bitcast_fusion.1
  300.6 22.0 %all_to_all.42 = f32[64,8,2,128]{3,2,1,0:T(2,128)S(1)} all-to-all(f32[64,8,2,128]{3,2,1,0:T(2,128)S(1)} %copy.107), channel_id=1, replica_groups=mesh['row_0'=8,'row_1'=4,'col_0'=8,'col_1'=2] {'row_1','col_0','col_1'}, dimensions={0} | all-to-all | bytes 1048576 | tf_op jit(solution)/shard_map/all_to_all | solution.py:24
  322.8 8.9 %all_to_all.43 = f32[8,2,128]{2,1,0:T(2,128)S(1)} all-to-all(f32[8,2,128]{2,1,0:T(2,128)S(1)} %reduce_sum.39), channel_id=1, replica_groups=mesh['row_0'=8,'row_1'=4,'col_0'=8,'col_1'=2] {'row_0'}, dimensions={0} | all-to-all | bytes 16384 | tf_op jit(solution)/shard_map/all_to_all | solution.py:46
  331.8 8.9 %all_to_all.40 = f32[8,2,128]{2,1,0:T(2,128)S(1)} all-to-all(f32[8,2,128]{2,1,0:T(2,128)S(1)} %broadcast_in_dim.75), channel_id=1, replica_groups=mesh['row_0'=8,'row_1'=4,'col_0'=8,'col_1'=2] {'row_0'}, dimensions={0} | all-to-all | bytes 16384 | tf_op jit(solution)/shard_map/all_to_all | solution.py:36
  340.7 0.9 broadcast_in_dim.76
  341.6 8.7 %all-to-all-start.5 = ((f32[64,8,2,128]{3,2,1,0:T(2,128)}), f32[64,8,2,128]{3,2,1,0:T(2,128)S(1)}, u32[]{:S(2)}, u32[]{:S(2)}) async-start(f32[64,8,2,128]{3,2,1,0:T(2,128)} %broadcast_in_dim.76), calls=%async_computation.5 | async-start | bytes 1048576 | tf_op jit(solution)/shard_map/all_to_all | solution.py:36
  350.7 17.0 %all-to-all-done.5 = f32[64,8,2,128]{3,2,1,0:T(2,128)S(1)} async-done(((f32[64,8,2,128]{3,2,1,0:T(2,128)}), f32[64,8,2,128]{3,2,1,0:T(2,128)S(1)}, u32[]{:S(2)}, u32[]{:S(2)}) %all-to-all-start.5) | async-done | bytes 524320 | tf_op jit(solution)/shard_map/all_to_all | solution.py:36
  367.7 0.9 while.56
  370.5 34.3 %all-gather.2.cloned.1.call-done = bf16[1024,4,128]{0,2,1:T(8,128)(2,1)} async-done(((bf16[1024,4,8]{0,2,1:T(8,128)(2,1)}), bf16[1024,4,128]{0,2,1:T(8,128)(2,1)}) %all-gather.2.cloned.1.call-update) | async-done | bytes 1048592 | tf_op jit(solution)/shard_map/all_gather | solution.py:159
  404.8 4.0 multiply_reduce_fusion
  408.8 14.1 %psum.28 = f32[]{:T(128)} all-reduce(f32[]{:T(128)} %get-tuple-element.519), channel_id=1, replica_groups=mesh['row_0'=8,'row_1'=4,'col_0'=8,'col_1'=2] {'row_0'}, use_global_device_ids=true, to_apply=%region_10.11 | all-reduce | flops 1 | bytes 8 | tf_op jit(solution)/shard_map/psum | solution.py:70
  422.9 9.0 %psum.29 = f32[]{:T(128)} all-reduce(f32[]{:T(128)} %psum.28), channel_id=1, replica_groups=mesh['row_0'=8,'row_1'=4,'col_0'=8,'col_1'=2] {'row_1'}, use_global_device_ids=true, to_apply=%region_11.12 | all-reduce | flops 1 | bytes 8 | tf_op jit(solution)/shard_map/psum | solution.py:70
  431.9 12.4 %psum.30 = f32[]{:T(128)} all-reduce(f32[]{:T(128)} %psum.29), channel_id=1, replica_groups=mesh['row_0'=8,'row_1'=4,'col_0'=8,'col_1'=2] {'col_0'}, use_global_device_ids=true, to_apply=%region_12.13 | all-reduce | flops 1 | bytes 8 | tf_op jit(solution)/shard_map/psum | solution.py:70
  444.2 12.3 %psum.31 = f32[]{:T(128)} all-reduce(f32[]{:T(128)} %psum.30), channel_id=1, replica_groups=mesh['row_0'=8,'row_1'=4,'col_0'=8,'col_1'=2] {'col_1'}, use_global_device_ids=true, to_apply=%region_13.14 | all-reduce | flops 1 | bytes 8 | tf_op jit(solution)/shard_map/psum | solution.py:70
  457.4 2.7 copy.116
  (148 shorter events, 25.5 us)
Async XLA Ops:
  7.2 2.4 copy-start
  7.2 2.7 copy-start.1
  9.9 0.8 copy-start.5
  9.9 0.8 copy-start.6
  34.0 24.5 %all-to-all-start.1 = ((f32[16,128,4,8]{1,3,2,0:T(8,128)}), f32[16,128,4,8]{1,3,2,0:T(8,128)S(1)}, u32[]{:S(2)}, u32[]{:S(2)}) async-start(f32[16,128,4,8]{1,3,2,0:T(8,128)} %copy.144), calls=%async_computation.1 | async-start | bytes 524288 | tf_op jit(solution)/shard_map/while/body/eval_jaxpr/all_to_all | solution.py:24
  76.7 15.9 %all-to-all-start.1 = ((f32[16,128,4,8]{1,3,2,0:T(8,128)}), f32[16,128,4,8]{1,3,2,0:T(8,128)S(1)}, u32[]{:S(2)}, u32[]{:S(2)}) async-start(f32[16,128,4,8]{1,3,2,0:T(8,128)} %copy.144), calls=%async_computation.1 | async-start | bytes 524288 | tf_op jit(solution)/shard_map/while/body/eval_jaxpr/all_to_all | solution.py:24
  111.0 15.6 %all-to-all-start.1 = ((f32[16,128,4,8]{1,3,2,0:T(8,128)}), f32[16,128,4,8]{1,3,2,0:T(8,128)S(1)}, u32[]{:S(2)}, u32[]{:S(2)}) async-start(f32[16,128,4,8]{1,3,2,0:T(8,128)} %copy.144), calls=%async_computation.1 | async-start | bytes 524288 | tf_op jit(solution)/shard_map/while/body/eval_jaxpr/all_to_all | solution.py:24
  145.2 15.6 %all-to-all-start.1 = ((f32[16,128,4,8]{1,3,2,0:T(8,128)}), f32[16,128,4,8]{1,3,2,0:T(8,128)S(1)}, u32[]{:S(2)}, u32[]{:S(2)}) async-start(f32[16,128,4,8]{1,3,2,0:T(8,128)} %copy.144), calls=%async_computation.1 | async-start | bytes 524288 | tf_op jit(solution)/shard_map/while/body/eval_jaxpr/all_to_all | solution.py:24
  179.4 15.6 %all-to-all-start.1 = ((f32[16,128,4,8]{1,3,2,0:T(8,128)}), f32[16,128,4,8]{1,3,2,0:T(8,128)S(1)}, u32[]{:S(2)}, u32[]{:S(2)}) async-start(f32[16,128,4,8]{1,3,2,0:T(8,128)} %copy.144), calls=%async_computation.1 | async-start | bytes 524288 | tf_op jit(solution)/shard_map/while/body/eval_jaxpr/all_to_all | solution.py:24
  213.6 15.6 %all-to-all-start.1 = ((f32[16,128,4,8]{1,3,2,0:T(8,128)}), f32[16,128,4,8]{1,3,2,0:T(8,128)S(1)}, u32[]{:S(2)}, u32[]{:S(2)}) async-start(f32[16,128,4,8]{1,3,2,0:T(8,128)} %copy.144), calls=%async_computation.1 | async-start | bytes 524288 | tf_op jit(solution)/shard_map/while/body/eval_jaxpr/all_to_all | solution.py:24
  247.8 15.6 %all-to-all-start.1 = ((f32[16,128,4,8]{1,3,2,0:T(8,128)}), f32[16,128,4,8]{1,3,2,0:T(8,128)S(1)}, u32[]{:S(2)}, u32[]{:S(2)}) async-start(f32[16,128,4,8]{1,3,2,0:T(8,128)} %copy.144), calls=%async_computation.1 | async-start | bytes 524288 | tf_op jit(solution)/shard_map/while/body/eval_jaxpr/all_to_all | solution.py:24
  282.0 15.6 %all-to-all-start.1 = ((f32[16,128,4,8]{1,3,2,0:T(8,128)}), f32[16,128,4,8]{1,3,2,0:T(8,128)S(1)}, u32[]{:S(2)}, u32[]{:S(2)}) async-start(f32[16,128,4,8]{1,3,2,0:T(8,128)} %copy.144), calls=%async_computation.1 | async-start | bytes 524288 | tf_op jit(solution)/shard_map/while/body/eval_jaxpr/all_to_all | solution.py:24
  300.2 50.2 %copy-start.4 = (bf16[128,4,128]{2,1,0:T(4,128)(2,1)S(1)}, bf16[128,4,128]{2,1,0:T(4,128)(2,1)}, u32[]{:S(2)}) copy-start(bf16[128,4,128]{2,1,0:T(4,128)(2,1)} %param.21) | copy-start | bytes 393220
  341.6 27.0 %copy-start.2 = (s32[8,128,128]{2,1,0:T(8,128)S(1)}, s32[8,128,128]{2,1,0:T(8,128)}, u32[]{:S(2)}) copy-start(s32[8,128,128]{2,1,0:T(8,128)} %param.16) | copy-start | bytes 1572868
  341.6 26.0 %all-to-all-start.5 = ((f32[64,8,2,128]{3,2,1,0:T(2,128)}), f32[64,8,2,128]{3,2,1,0:T(2,128)S(1)}, u32[]{:S(2)}, u32[]{:S(2)}) async-start(f32[64,8,2,128]{3,2,1,0:T(2,128)} %broadcast_in_dim.76), calls=%async_computation.5 | async-start | bytes 1048576 | tf_op jit(solution)/shard_map/all_to_all | solution.py:36
  350.3 54.5 %all-gather.2.cloned.1.call-start = ((), (), s32[]{:S(2)}) async-start(), calls=%async_computation.6 | async-start | bytes 1114112 | tf_op jit(solution)/shard_map/all_gather | solution.py:159
  368.6 1.9 copy-start.3
Sparse Core Ops, SparseCore 0:
  370.7 34.1 all-gather.1
where the time goes:
time: 469 us; the launch traced here: 467 us
  blocking collectives  226 us (48%)
  waiting for transfers between devices  136 us (29%)
  starting transfers between devices  47.9 us (10%)
  local copies, waits for them, and re-layouts  22 us (5%)
  between operations  15 us (3%)
  matrix products  10.9 us (2%)
  other arithmetic  7.65 us (2%)
    all_to_all x9, blocking collectives, sent_to_all(): return lax.all_to_all(copies, axis, split_axis=0, concat_axis=0, tiled=True)  148 us
    all_to_all x8, waiting for transfers between devices, sum_at_owner(): lax.all_to_all(cut_along(array, dim, length), axis, 0, 0, tiled=True)  84.7 us
    psum x4, blocking collectives, by_axis(): return functools.reduce(lax.psum, axes, array)  47.7 us
    all_to_all x8, starting transfers between devices, sum_at_owner(): lax.all_to_all(cut_along(array, dim, length), axis, 0, 0, tiled=True)  39.1 us
    all_gather x1, waiting for transfers between devices, body(): lax.all_gather(factors.reshape(rows_all, rows_loc, state_cols), COL, axis...  34.3 us
    all_to_all x1, blocking collectives, sum_at_owner(): lax.all_to_all(cut_along(array, dim, length), axis, 0, 0, tiled=True)  22 us
    all_to_all x1, waiting for transfers between devices, sent_to_all(): return lax.all_to_all(copies, axis, split_axis=0, concat_axis=0, tiled=True)  17 us
  transfers between devices with their start and end apart: 10, of which 10 were waited for; matrix products, arithmetic and copies ran while one was open for 2% of the time, Pallas kernels for 0%

commit v1 on v0

--- a/solution.py
+++ b/solution.py
@@ -156,8 +156,14 @@
     _, future = lax.scan(backward, zeros, (weighted, decays), reverse=True)
     factors = (weighted - coupling_magnitude * slopes * future).astype(jnp.bfloat16)
     traces_flat = traces.reshape(rows_all, -1)
-    pieces = lax.all_gather(
-        factors.reshape(rows_all, rows_loc, state_cols), COL, axis=2, tiled=True
+    pieces = jnp.concatenate(
+        lax.all_to_all(
+            jnp.stack([factors.reshape(rows_all, rows_loc, state_cols)] * lax.axis_size(COL)),
+            COL,
+            0,
+            0,
+        ),
+        axis=2,
     )
     product = lax.dot_general(
         traces_flat,

time: 469 us -> 446 us (0.951)
  waiting for transfers between devices: 136 us -> 102 us
  blocking collectives: 226 us -> 253 us
  between operations: 15 us -> 1.67 us
    all_gather x1 -> x0, waiting for transfers between devices: 34.3 us -> none  [body(): lax.all_gather(factors.reshape(rows_all, rows_loc, state_cols), COL, axis...]
    all_to_all x0 -> x1, blocking collectives: none -> 33.2 us  [body(): lax.all_to_all(jnp.stack([factors.reshape(rows_all, rows_loc, state_cols)...]
    psum x4, blocking collectives: 47.7 us -> 41.5 us  [by_axis(): return functools.reduce(lax.psum, axes, array)]
  transfers between devices with their start and end apart: 10 -> 9, of which waited for: 10 -> 9; matrix products, arithmetic and copies ran while one was open for 2% -> 2% of each run, Pallas kernels for 0% -> 0%
where the time goes in v1:
time: 446 us; the launch traced here: 444 us
  blocking collectives  253 us (57%)
  waiting for transfers between devices  102 us (23%)
  starting transfers between devices  47.8 us (11%)
  local copies, waits for them, and re-layouts  22.2 us (5%)
  matrix products  9.13 us (2%)
  other arithmetic  7.03 us (2%)
    all_to_all x9, blocking collectives, sent_to_all(): return lax.all_to_all(copies, axis, split_axis=0, concat_axis=0, tiled=True)  148 us
    all_to_all x8, waiting for transfers between devices, sum_at_owner(): lax.all_to_all(cut_along(array, dim, length), axis, 0, 0, tiled=True)  84.7 us
    psum x4, blocking collectives, by_axis(): return functools.reduce(lax.psum, axes, array)  41.5 us
    all_to_all x8, starting transfers between devices, sum_at_owner(): lax.all_to_all(cut_along(array, dim, length), axis, 0, 0, tiled=True)  39.1 us
    all_to_all x1, blocking collectives, body(): lax.all_to_all(jnp.stack([factors.reshape(rows_all, rows_loc, state_cols)...  33.2 us
    all_to_all x1, blocking collectives, sum_at_owner(): lax.all_to_all(cut_along(array, dim, length), axis, 0, 0, tiled=True)  22 us
    all_to_all x1, waiting for transfers between devices, sent_to_all(): return lax.all_to_all(copies, axis, split_axis=0, concat_axis=0, tiled=True)  17.1 us
    all_to_all x1, blocking collectives, summed_rows(): return jnp.sum(lax.all_to_all(own, far, 0, 0, tiled=True), axis=0)  8.92 us
  transfers between devices with their start and end apart: 9, of which 9 were waited for; matrix products, arithmetic and copies ran while one was open for 2% of the time, Pallas kernels for 0%

profile of v1, /device:TPU:1, one launch (start us, length us, event | category | flops | bytes accessed | tf_op | source)
XLA Modules:
  0.0 443.9 jit_solution(5757415619505345226)
XLA Ops:
  0.7 1.1 constant_dynamic-slice_fusion.4
  1.9 1.1 convert_element_type.57
  4.4 286.9 %while.55 = (s32[]{:T(128)}, bf16[128,4,8]{0,2,1:T(8,128)(2,1)S(1)}, f32[128,4,8]{0,2,1:T(8,128)S(1)}, f32[128,4,8]{0,2,1:T(8,128)S(1)}, f32[128,1024]{0,1:T(8,1...) while((s32[]{:T(128)}, ...), condition=%wide.region_2.3_spmd.clone, body=%wide.region_0.2_spmd.clone.sunk | while | flops 135032832 | bytes 6756560 | solution.py:125
  4.5 21.5 %all_to_all.47 = bf16[32,128,4,8]{1,3,2,0:T(8,128)(2,1)S(1)} all-to-all(bf16[32,128,4,8]{1,3,2,0:T(8,128)(2,1)S(1)} %broadcast_in_dim.84), channel_id=1, replica_groups=mesh['row_0'=8,'row_1'=4,'col_0'=8,'col_1'=2] {'row_0','row_1'}, dimensions={0} | all-to-all | bytes 524288 | tf_op jit(solution)/shard_map/while/body/eval_jaxpr/all_to_all | solution.py:36
  26.7 0.8 copy.153
  27.5 12.8 %all-to-all-start.1 = ((f32[16,128,4,8]{1,3,2,0:T(8,128)}), f32[16,128,4,8]{1,3,2,0:T(8,128)S(1)}, u32[]{:S(2)}, u32[]{:S(2)}) async-start(f32[16,128,4,8]{1,3,2,0:T(8,128)} %copy.153), calls=%async_computation.1 | async-start | bytes 524288 | tf_op jit(solution)/shard_map/while/body/eval_jaxpr/all_to_all | solution.py:24
  41.5 10.5 %all-to-all-done.1 = f32[16,128,4,8]{1,3,2,0:T(8,128)S(1)} async-done(((f32[16,128,4,8]{1,3,2,0:T(8,128)}), f32[16,128,4,8]{1,3,2,0:T(8,128)S(1)}, u32[]{:S(2)}, u32[]{:S(2)}) %all-to-all-start.1) | async-done | bytes 262176 | tf_op jit(solution)/shard_map/while/body/eval_jaxpr/all_to_all | solution.py:24
  52.2 16.4 %all_to_all.47 = bf16[32,128,4,8]{1,3,2,0:T(8,128)(2,1)S(1)} all-to-all(bf16[32,128,4,8]{1,3,2,0:T(8,128)(2,1)S(1)} %broadcast_in_dim.84), channel_id=1, replica_groups=mesh['row_0'=8,'row_1'=4,'col_0'=8,'col_1'=2] {'row_0','row_1'}, dimensions={0} | all-to-all | bytes 524288 | tf_op jit(solution)/shard_map/while/body/eval_jaxpr/all_to_all | solution.py:36
  69.4 0.8 copy.153
  70.2 4.0 all-to-all-start.1
  75.4 10.6 %all-to-all-done.1 = f32[16,128,4,8]{1,3,2,0:T(8,128)S(1)} async-done(((f32[16,128,4,8]{1,3,2,0:T(8,128)}), f32[16,128,4,8]{1,3,2,0:T(8,128)S(1)}, u32[]{:S(2)}, u32[]{:S(2)}) %all-to-all-start.1) | async-done | bytes 262176 | tf_op jit(solution)/shard_map/while/body/eval_jaxpr/all_to_all | solution.py:24
  86.3 16.7 %all_to_all.47 = bf16[32,128,4,8]{1,3,2,0:T(8,128)(2,1)S(1)} all-to-all(bf16[32,128,4,8]{1,3,2,0:T(8,128)(2,1)S(1)} %broadcast_in_dim.84), channel_id=1, replica_groups=mesh['row_0'=8,'row_1'=4,'col_0'=8,'col_1'=2] {'row_0','row_1'}, dimensions={0} | all-to-all | bytes 524288 | tf_op jit(solution)/shard_map/while/body/eval_jaxpr/all_to_all | solution.py:36
  103.7 0.8 copy.153
  104.5 3.7 all-to-all-start.1
  109.5 10.6 %all-to-all-done.1 = f32[16,128,4,8]{1,3,2,0:T(8,128)S(1)} async-done(((f32[16,128,4,8]{1,3,2,0:T(8,128)}), f32[16,128,4,8]{1,3,2,0:T(8,128)S(1)}, u32[]{:S(2)}, u32[]{:S(2)}) %all-to-all-start.1) | async-done | bytes 262176 | tf_op jit(solution)/shard_map/while/body/eval_jaxpr/all_to_all | solution.py:24
  120.4 16.9 %all_to_all.47 = bf16[32,128,4,8]{1,3,2,0:T(8,128)(2,1)S(1)} all-to-all(bf16[32,128,4,8]{1,3,2,0:T(8,128)(2,1)S(1)} %broadcast_in_dim.84), channel_id=1, replica_groups=mesh['row_0'=8,'row_1'=4,'col_0'=8,'col_1'=2] {'row_0','row_1'}, dimensions={0} | all-to-all | bytes 524288 | tf_op jit(solution)/shard_map/while/body/eval_jaxpr/all_to_all | solution.py:36
  137.9 0.8 copy.153
  138.7 3.7 all-to-all-start.1
  143.7 10.6 %all-to-all-done.1 = f32[16,128,4,8]{1,3,2,0:T(8,128)S(1)} async-done(((f32[16,128,4,8]{1,3,2,0:T(8,128)}), f32[16,128,4,8]{1,3,2,0:T(8,128)S(1)}, u32[]{:S(2)}, u32[]{:S(2)}) %all-to-all-start.1) | async-done | bytes 262176 | tf_op jit(solution)/shard_map/while/body/eval_jaxpr/all_to_all | solution.py:24
  154.6 16.9 %all_to_all.47 = bf16[32,128,4,8]{1,3,2,0:T(8,128)(2,1)S(1)} all-to-all(bf16[32,128,4,8]{1,3,2,0:T(8,128)(2,1)S(1)} %broadcast_in_dim.84), channel_id=1, replica_groups=mesh['row_0'=8,'row_1'=4,'col_0'=8,'col_1'=2] {'row_0','row_1'}, dimensions={0} | all-to-all | bytes 524288 | tf_op jit(solution)/shard_map/while/body/eval_jaxpr/all_to_all | solution.py:36
  172.1 0.8 copy.153
  172.9 3.7 all-to-all-start.1
  177.9 10.6 %all-to-all-done.1 = f32[16,128,4,8]{1,3,2,0:T(8,128)S(1)} async-done(((f32[16,128,4,8]{1,3,2,0:T(8,128)}), f32[16,128,4,8]{1,3,2,0:T(8,128)S(1)}, u32[]{:S(2)}, u32[]{:S(2)}) %all-to-all-start.1) | async-done | bytes 262176 | tf_op jit(solution)/shard_map/while/body/eval_jaxpr/all_to_all | solution.py:24
  188.8 16.9 %all_to_all.47 = bf16[32,128,4,8]{1,3,2,0:T(8,128)(2,1)S(1)} all-to-all(bf16[32,128,4,8]{1,3,2,0:T(8,128)(2,1)S(1)} %broadcast_in_dim.84), channel_id=1, replica_groups=mesh['row_0'=8,'row_1'=4,'col_0'=8,'col_1'=2] {'row_0','row_1'}, dimensions={0} | all-to-all | bytes 524288 | tf_op jit(solution)/shard_map/while/body/eval_jaxpr/all_to_all | solution.py:36
  207.1 3.7 all-to-all-start.1
  212.1 10.6 %all-to-all-done.1 = f32[16,128,4,8]{1,3,2,0:T(8,128)S(1)} async-done(((f32[16,128,4,8]{1,3,2,0:T(8,128)}), f32[16,128,4,8]{1,3,2,0:T(8,128)S(1)}, u32[]{:S(2)}, u32[]{:S(2)}) %all-to-all-start.1) | async-done | bytes 262176 | tf_op jit(solution)/shard_map/while/body/eval_jaxpr/all_to_all | solution.py:24
  223.0 16.9 %all_to_all.47 = bf16[32,128,4,8]{1,3,2,0:T(8,128)(2,1)S(1)} all-to-all(bf16[32,128,4,8]{1,3,2,0:T(8,128)(2,1)S(1)} %broadcast_in_dim.84), channel_id=1, replica_groups=mesh['row_0'=8,'row_1'=4,'col_0'=8,'col_1'=2] {'row_0','row_1'}, dimensions={0} | all-to-all | bytes 524288 | tf_op jit(solution)/shard_map/while/body/eval_jaxpr/all_to_all | solution.py:36
  241.3 3.7 all-to-all-start.1
  246.3 10.6 %all-to-all-done.1 = f32[16,128,4,8]{1,3,2,0:T(8,128)S(1)} async-done(((f32[16,128,4,8]{1,3,2,0:T(8,128)}), f32[16,128,4,8]{1,3,2,0:T(8,128)S(1)}, u32[]{:S(2)}, u32[]{:S(2)}) %all-to-all-start.1) | async-done | bytes 262176 | tf_op jit(solution)/shard_map/while/body/eval_jaxpr/all_to_all | solution.py:24
  257.2 16.9 %all_to_all.47 = bf16[32,128,4,8]{1,3,2,0:T(8,128)(2,1)S(1)} all-to-all(bf16[32,128,4,8]{1,3,2,0:T(8,128)(2,1)S(1)} %broadcast_in_dim.84), channel_id=1, replica_groups=mesh['row_0'=8,'row_1'=4,'col_0'=8,'col_1'=2] {'row_0','row_1'}, dimensions={0} | all-to-all | bytes 524288 | tf_op jit(solution)/shard_map/while/body/eval_jaxpr/all_to_all | solution.py:36
  275.5 3.7 all-to-all-start.1
  280.5 10.6 %all-to-all-done.1 = f32[16,128,4,8]{1,3,2,0:T(8,128)S(1)} async-done(((f32[16,128,4,8]{1,3,2,0:T(8,128)}), f32[16,128,4,8]{1,3,2,0:T(8,128)S(1)}, u32[]{:S(2)}, u32[]{:S(2)}) %all-to-all-start.1) | async-done | bytes 262176 | tf_op jit(solution)/shard_map/while/body/eval_jaxpr/all_to_all | solution.py:24
  291.3 0.9 copy.107
  292.8 0.9 convolution_bitcast_fusion.1
  294.1 22.0 %all_to_all.48 = f32[64,8,2,128]{3,2,1,0:T(2,128)S(1)} all-to-all(f32[64,8,2,128]{3,2,1,0:T(2,128)S(1)} %copy.109), channel_id=1, replica_groups=mesh['row_0'=8,'row_1'=4,'col_0'=8,'col_1'=2] {'row_1','col_0','col_1'}, dimensions={0} | all-to-all | bytes 1048576 | tf_op jit(solution)/shard_map/all_to_all | solution.py:24
  316.3 8.9 %all_to_all.49 = f32[8,2,128]{2,1,0:T(2,128)S(1)} all-to-all(f32[8,2,128]{2,1,0:T(2,128)S(1)} %reduce_sum.39), channel_id=1, replica_groups=mesh['row_0'=8,'row_1'=4,'col_0'=8,'col_1'=2] {'row_0'}, dimensions={0} | all-to-all | bytes 16384 | tf_op jit(solution)/shard_map/all_to_all | solution.py:46
  325.2 8.9 %all_to_all.45 = f32[8,2,128]{2,1,0:T(2,128)S(1)} all-to-all(f32[8,2,128]{2,1,0:T(2,128)S(1)} %broadcast_in_dim.75), channel_id=1, replica_groups=mesh['row_0'=8,'row_1'=4,'col_0'=8,'col_1'=2] {'row_0'}, dimensions={0} | all-to-all | bytes 16384 | tf_op jit(solution)/shard_map/all_to_all | solution.py:36
  334.2 0.9 broadcast_in_dim.76
  335.1 8.7 %all-to-all-start.5 = ((f32[64,8,2,128]{3,2,1,0:T(2,128)}), f32[64,8,2,128]{3,2,1,0:T(2,128)S(1)}, u32[]{:S(2)}, u32[]{:S(2)}) async-start(f32[64,8,2,128]{3,2,1,0:T(2,128)} %broadcast_in_dim.76), calls=%async_computation.5 | async-start | bytes 1048576 | tf_op jit(solution)/shard_map/all_to_all | solution.py:36
  344.1 17.1 %all-to-all-done.5 = f32[64,8,2,128]{3,2,1,0:T(2,128)S(1)} async-done(((f32[64,8,2,128]{3,2,1,0:T(2,128)}), f32[64,8,2,128]{3,2,1,0:T(2,128)S(1)}, u32[]{:S(2)}, u32[]{:S(2)}) %all-to-all-start.5) | async-done | bytes 524320 | tf_op jit(solution)/shard_map/all_to_all | solution.py:36
  361.2 0.9 while.56
  363.5 33.2 %all_to_all.46 = bf16[16,1024,4,8]{1,3,2,0:T(8,128)(2,1)S(1)} all-to-all(bf16[16,1024,4,8]{1,3,2,0:T(8,128)(2,1)S(1)} %stack.3), channel_id=1, replica_groups=mesh['row_0'=8,'row_1'=4,'col_0'=8,'col_1'=2] {'col_0','col_1'}, dimensions={0} | all-to-all | bytes 2097152 | tf_op jit(solution)/shard_map/all_to_all | solution.py:160
  396.7 2.2 multiply_reduce_fusion
  398.9 11.6 %psum.28 = f32[]{:T(128)} all-reduce(f32[]{:T(128)} %get-tuple-element.519), channel_id=1, replica_groups=mesh['row_0'=8,'row_1'=4,'col_0'=8,'col_1'=2] {'row_0'}, use_global_device_ids=true, to_apply=%region_10.11 | all-reduce | flops 1 | bytes 8 | tf_op jit(solution)/shard_map/psum | solution.py:70
  410.5 7.3 %psum.29 = f32[]{:T(128)} all-reduce(f32[]{:T(128)} %psum.28), channel_id=1, replica_groups=mesh['row_0'=8,'row_1'=4,'col_0'=8,'col_1'=2] {'row_1'}, use_global_device_ids=true, to_apply=%region_11.12 | all-reduce | flops 1 | bytes 8 | tf_op jit(solution)/shard_map/psum | solution.py:70
  417.7 11.3 %psum.30 = f32[]{:T(128)} all-reduce(f32[]{:T(128)} %psum.29), channel_id=1, replica_groups=mesh['row_0'=8,'row_1'=4,'col_0'=8,'col_1'=2] {'col_0'}, use_global_device_ids=true, to_apply=%region_12.13 | all-reduce | flops 1 | bytes 8 | tf_op jit(solution)/shard_map/psum | solution.py:70
  429.0 11.4 %psum.31 = f32[]{:T(128)} all-reduce(f32[]{:T(128)} %psum.30), channel_id=1, replica_groups=mesh['row_0'=8,'row_1'=4,'col_0'=8,'col_1'=2] {'col_1'}, use_global_device_ids=true, to_apply=%region_13.14 | all-reduce | flops 1 | bytes 8 | tf_op jit(solution)/shard_map/psum | solution.py:70
  441.3 2.7 copy.119
  (149 shorter events, 24.9 us)
Async XLA Ops:
  0.6 2.4 copy-start
  0.6 2.7 copy-start.1
  3.4 0.8 copy-start.5
  3.4 0.8 copy-start.6
  27.5 24.5 %all-to-all-start.1 = ((f32[16,128,4,8]{1,3,2,0:T(8,128)}), f32[16,128,4,8]{1,3,2,0:T(8,128)S(1)}, u32[]{:S(2)}, u32[]{:S(2)}) async-start(f32[16,128,4,8]{1,3,2,0:T(8,128)} %copy.153), calls=%async_computation.1 | async-start | bytes 524288 | tf_op jit(solution)/shard_map/while/body/eval_jaxpr/all_to_all | solution.py:24
  70.2 15.9 %all-to-all-start.1 = ((f32[16,128,4,8]{1,3,2,0:T(8,128)}), f32[16,128,4,8]{1,3,2,0:T(8,128)S(1)}, u32[]{:S(2)}, u32[]{:S(2)}) async-start(f32[16,128,4,8]{1,3,2,0:T(8,128)} %copy.153), calls=%async_computation.1 | async-start | bytes 524288 | tf_op jit(solution)/shard_map/while/body/eval_jaxpr/all_to_all | solution.py:24
  104.5 15.6 %all-to-all-start.1 = ((f32[16,128,4,8]{1,3,2,0:T(8,128)}), f32[16,128,4,8]{1,3,2,0:T(8,128)S(1)}, u32[]{:S(2)}, u32[]{:S(2)}) async-start(f32[16,128,4,8]{1,3,2,0:T(8,128)} %copy.153), calls=%async_computation.1 | async-start | bytes 524288 | tf_op jit(solution)/shard_map/while/body/eval_jaxpr/all_to_all | solution.py:24
  138.7 15.6 %all-to-all-start.1 = ((f32[16,128,4,8]{1,3,2,0:T(8,128)}), f32[16,128,4,8]{1,3,2,0:T(8,128)S(1)}, u32[]{:S(2)}, u32[]{:S(2)}) async-start(f32[16,128,4,8]{1,3,2,0:T(8,128)} %copy.153), calls=%async_computation.1 | async-start | bytes 524288 | tf_op jit(solution)/shard_map/while/body/eval_jaxpr/all_to_all | solution.py:24
  172.9 15.6 %all-to-all-start.1 = ((f32[16,128,4,8]{1,3,2,0:T(8,128)}), f32[16,128,4,8]{1,3,2,0:T(8,128)S(1)}, u32[]{:S(2)}, u32[]{:S(2)}) async-start(f32[16,128,4,8]{1,3,2,0:T(8,128)} %copy.153), calls=%async_computation.1 | async-start | bytes 524288 | tf_op jit(solution)/shard_map/while/body/eval_jaxpr/all_to_all | solution.py:24
  207.1 15.6 %all-to-all-start.1 = ((f32[16,128,4,8]{1,3,2,0:T(8,128)}), f32[16,128,4,8]{1,3,2,0:T(8,128)S(1)}, u32[]{:S(2)}, u32[]{:S(2)}) async-start(f32[16,128,4,8]{1,3,2,0:T(8,128)} %copy.153), calls=%async_computation.1 | async-start | bytes 524288 | tf_op jit(solution)/shard_map/while/body/eval_jaxpr/all_to_all | solution.py:24
  241.3 15.6 %all-to-all-start.1 = ((f32[16,128,4,8]{1,3,2,0:T(8,128)}), f32[16,128,4,8]{1,3,2,0:T(8,128)S(1)}, u32[]{:S(2)}, u32[]{:S(2)}) async-start(f32[16,128,4,8]{1,3,2,0:T(8,128)} %copy.153), calls=%async_computation.1 | async-start | bytes 524288 | tf_op jit(solution)/shard_map/while/body/eval_jaxpr/all_to_all | solution.py:24
  275.5 15.6 %all-to-all-start.1 = ((f32[16,128,4,8]{1,3,2,0:T(8,128)}), f32[16,128,4,8]{1,3,2,0:T(8,128)S(1)}, u32[]{:S(2)}, u32[]{:S(2)}) async-start(f32[16,128,4,8]{1,3,2,0:T(8,128)} %copy.153), calls=%async_computation.1 | async-start | bytes 524288 | tf_op jit(solution)/shard_map/while/body/eval_jaxpr/all_to_all | solution.py:24
  293.7 50.2 %copy-start.4 = (bf16[128,4,128]{2,1,0:T(4,128)(2,1)S(1)}, bf16[128,4,128]{2,1,0:T(4,128)(2,1)}, u32[]{:S(2)}) copy-start(bf16[128,4,128]{2,1,0:T(4,128)(2,1)} %param.21) | copy-start | bytes 393220
  335.1 27.0 %copy-start.2 = (s32[8,128,128]{2,1,0:T(8,128)S(1)}, s32[8,128,128]{2,1,0:T(8,128)}, u32[]{:S(2)}) copy-start(s32[8,128,128]{2,1,0:T(8,128)} %param.16) | copy-start | bytes 1572868
  335.1 26.0 %all-to-all-start.5 = ((f32[64,8,2,128]{3,2,1,0:T(2,128)}), f32[64,8,2,128]{3,2,1,0:T(2,128)S(1)}, u32[]{:S(2)}, u32[]{:S(2)}) async-start(f32[64,8,2,128]{3,2,1,0:T(2,128)} %broadcast_in_dim.76), calls=%async_computation.5 | async-start | bytes 1048576 | tf_op jit(solution)/shard_map/all_to_all | solution.py:36
  362.1 1.3 copy-start.3
  363.3 33.4 %copy-start.7 = (bf16[8,128,1024]{2,1,0:T(8,128)(2,1)S(1)}, bf16[8,128,1024]{2,1,0:T(8,128)(2,1)}, u32[]{:S(2)}) copy-start(bf16[8,128,1024]{2,1,0:T(8,128)(2,1)} %get-tuple-element.280) | copy-start | bytes 6291460
